TPU v7x, 32 devices: a whole 2x2x4 slice. The times are simulated.
32 devices in a mesh: grp: 2 (over y), con: 4 (over z), rep: 2 (over x), sub: 2 (over core).
Axes of the slice: x: 2, y: 2, z: 4, core: 2. Of those that a mesh axis runs over, the one named last changes fastest.
Arguments:
- integrals: float32 [512, 9600], P(('grp', 'con'), ('rep', 'sub')), parts along dimension 0, as said below
- ladder: float32 [19200, 9600], P(('grp', 'con'), ('rep', 'sub')), parts along dimension 0, may hold values from -0.1875 to 0.1875
- pair_energy: float32 [512], P(('grp', 'con')), parts along dimension 0, may hold values from -3 to -1
- virt_energy: float32 [19200], P(('grp', 'rep', 'sub')), parts along dimension 0, may hold values from 0.5 to 3
- pair_irrep: int32 [512], P('grp'), parts along dimension 0, may hold values from 0 to 7, as said below
- virt_irrep: int32 [19200], P('grp'), parts along dimension 0, may hold values from 0 to 7, as said below
Outputs:
- amplitude: float32 [512, 9600], P(('grp', 'con'), ('rep', 'sub')), parts along dimension 0
There are 2 independent parts, one for each index of `grp`. A program takes and returns all parts, laid end to end along the dimension named above; each array names one. Nothing has to cross between parts.
Inputs may be any that keep to these rules, and one draw needn't show every extreme that they name: `pair_irrep`: sorted ascending; the rows of one label form one run of at most 48 rows, and some label has exactly 48. `virt_irrep`: sorted ascending within each aligned block of 2400 virtual pairs; a label holds at most 600 virtual pairs of a block, and in every block some label holds exactly 600. `integrals`: zero wherever the row's pair_irrep differs from the column's virt_irrep.
All inputs are finite; a program needn't handle non-finite values.
Results may differ from a plain program's by a relative error of at most 0.0001.
Values sent between devices are 32-bit elements; how exact they have to be, the bound alone decides.
A program may use at most 192 MiB of HBM per device.

v0:
```python
import jax
import jax.numpy as jnp
from jax import lax
from jax.sharding import PartitionSpec as P

ITERS = 2


def per_device(integrals, ladder, pair_energy, virt_energy, pair_irrep, virt_irrep):
    row_count = integrals.shape[0]
    col_count = integrals.shape[1]
    con_index = lax.axis_index("con")
    rs_index = lax.axis_index(("rep", "sub"))
    groups = lax.axis_size(("rep", "sub"))
    pair_local = lax.dynamic_slice_in_dim(pair_irrep, con_index * row_count, row_count)
    virt_local = lax.dynamic_slice_in_dim(virt_irrep, rs_index * col_count, col_count)
    divisor = virt_energy[None, :] - pair_energy[:, None]
    allowed = pair_local[:, None] == virt_local[None, :]
    amplitude = integrals / divisor
    for repeat in range(ITERS):
        folded = amplitude.reshape(groups, row_count // groups, col_count)
        partial_value = jnp.einsum(
            "gmc,ac->gma",
            lax.all_gather(folded, "con", axis=1, tiled=True),
            ladder,
            precision=lax.Precision.HIGHEST,
            preferred_element_type=jnp.float32,
        )
        partial_value = partial_value.reshape(-1, partial_value.shape[-1])
        reduced = lax.psum_scatter(partial_value, ("rep", "sub"), scatter_dimension=0, tiled=True)
        ladder_term = lax.all_to_all(
            lax.all_to_all(reduced, "con", split_axis=0, concat_axis=1, tiled=True),
            ("rep", "sub"),
            split_axis=1,
            concat_axis=0,
            tiled=True,
        )
        amplitude = (
            integrals + jnp.where(allowed, ladder_term, jnp.zeros_like(ladder_term))
        ) / divisor
    return amplitude


def solution(mesh):
    in_specs = (
        P(("grp", "con"), ("rep", "sub")),
        P(("grp", "con"), ("rep", "sub")),
        P(("grp", "con")),
        P(("grp", "rep", "sub")),
        P("grp"),
        P("grp"),
    )
    out_specs = P(("grp", "con"), ("rep", "sub"))
    return jax.shard_map(
        per_device, mesh=mesh, in_specs=in_specs, out_specs=out_specs, check_vma=False
    )
```

profile of v0, /device:TPU:0, one launch (start us, length us, event | category | flops | bytes accessed | tf_op | source)
XLA Modules:
  0.0 311.2 jit_solution(14341900644042309623)
XLA Ops:
  6.5 2.1 subtract_divide_fusion.2
  8.6 0.0 all-gather.3.cloned.1.call-update
  8.6 0.0 reduce-scatter.3.cloned.1.call-start
  8.7 55.6 %all-gather.3.cloned.1.call-done = f32[4,64,2400]{2,1,0:T(8,128)} async-done(((f32[4,16,2400]{2,1,0:T(8,128)}), f32[4,64,2400]{2,1,0:T(8,128)}) %all-gather.3.cloned.1.call-update) | async-done | bytes 2457616 | tf_op jit(solution)/shard_map/all_gather | solution.py:24
  64.3 26.7 %fusion.2 = f32[4,64,2400]{2,1,0:T(8,128)} fusion(f32[4,64,2400]{2,1,0:T(8,128)} %all-gather.3.cloned.1.call-done, f32[2400,2400]{1,0:T(8,128)} %param.7), kind=kOutput, calls=%fused_computation.2 | convolution fusion | flops 17694720000 | bytes 27955200 | tf_op jit(solution)/shard_map/gmc,ac->gma/dot_general | solution.py:22
  91.0 0.0 copy-start.2
  91.0 0.0 reduce-scatter.3.cloned.1.call-update
  91.0 32.8 %reduce-scatter.3.cloned.1.call-done = f32[64,2400]{1,0:T(8,128)} async-done(((f32[256,2400]{1,0:T(8,128)}), f32[64,2400]{1,0:T(8,128)}) %reduce-scatter.3.cloned.1.call-update) | async-done | bytes 614416 | tf_op jit(solution)/shard_map/reduce_scatter | solution.py:30
  123.9 21.3 %all_to_all.64 = f32[4,16,2400]{2,1,0:T(8,128)} all-to-all(f32[4,16,2400]{2,1,0:T(8,128)} %bitcast.28), channel_id=1, replica_groups=mesh['grp'=2,'con'=4,'rep'=2,'sub'=2] {'con'}, dimensions={0} | all-to-all | bytes 1228800 | tf_op jit(solution)/shard_map/all_to_all | solution.py:32
  145.2 3.5 %all-to-all-start.1 = ((f32[16,4,2400]{2,0,1:T(8,128)}), f32[16,4,2400]{2,0,1:T(8,128)S(1)}, u32[]{:S(2)}, u32[]{:S(2)}) async-start(f32[16,4,2400]{2,0,1:T(8,128)} %bitcast.4), calls=%async_computation.2 | async-start | bytes 1245184 | tf_op jit(solution)/shard_map/all_to_all | solution.py:31
  148.7 0.0 all-gather.5.cloned.1.call-start
  148.7 0.1 dynamic_slice.6
  148.8 0.8 dynamic_slice.7
  149.6 8.9 %all-to-all-done.1 = f32[16,4,2400]{2,0,1:T(8,128)S(1)} async-done(((f32[16,4,2400]{2,0,1:T(8,128)}), f32[16,4,2400]{2,0,1:T(8,128)S(1)}, u32[]{:S(2)}, u32[]{:S(2)}) %all-to-all-start.1) | async-done | bytes 614432 | tf_op jit(solution)/shard_map/all_to_all | solution.py:31
  158.5 1.1 subtract_divide_fusion.1
  159.6 0.0 all-gather.5.cloned.1.call-update
  159.6 0.0 reduce-scatter.5.cloned.1.call-start
  159.7 50.9 %all-gather.5.cloned.1.call-done = f32[4,64,2400]{2,1,0:T(8,128)} async-done(((f32[4,16,2400]{2,1,0:T(8,128)}), f32[4,64,2400]{2,1,0:T(8,128)}) %all-gather.5.cloned.1.call-update) | async-done | bytes 2457616 | tf_op jit(solution)/shard_map/all_gather | solution.py:24
  210.5 26.7 %fusion = f32[4,64,2400]{2,1,0:T(8,128)} fusion(f32[4,64,2400]{2,1,0:T(8,128)} %all-gather.5.cloned.1.call-done, f32[2400,2400]{1,0:T(8,128)} %param.7), kind=kOutput, calls=%fused_computation | convolution fusion | flops 17694720000 | bytes 27955200 | tf_op jit(solution)/shard_map/gmc,ac->gma/dot_general | solution.py:22
  237.3 0.0 reduce-scatter.5.cloned.1.call-update
  237.3 32.8 %reduce-scatter.5.cloned.1.call-done = f32[64,2400]{1,0:T(8,128)} async-done(((f32[256,2400]{1,0:T(8,128)}), f32[64,2400]{1,0:T(8,128)}) %reduce-scatter.5.cloned.1.call-update) | async-done | bytes 614416 | tf_op jit(solution)/shard_map/reduce_scatter | solution.py:30
  270.1 21.2 %all_to_all.65 = f32[4,16,2400]{2,1,0:T(8,128)S(1)} all-to-all(f32[4,16,2400]{2,1,0:T(8,128)} %bitcast.29), channel_id=1, replica_groups=mesh['grp'=2,'con'=4,'rep'=2,'sub'=2] {'con'}, dimensions={0} | all-to-all | bytes 1228800 | tf_op jit(solution)/shard_map/all_to_all | solution.py:32
  291.3 12.3 %all_to_all.66 = f32[16,4,2400]{2,0,1:T(8,128)S(1)} all-to-all(f32[16,4,2400]{2,0,1:T(8,128)S(1)} %bitcast.27), channel_id=1, replica_groups=mesh['grp'=2,'con'=4,'rep'=2,'sub'=2] {'rep','sub'}, dimensions={1} | all-to-all | bytes 1228800 | tf_op jit(solution)/shard_map/all_to_all | solution.py:31
  303.6 1.0 subtract_divide_fusion
  (8 shorter events, 0.0 us)
Async XLA Ops:
  6.5 57.7 %all-gather.3.cloned.1.call-start = ((), (), s32[]{:S(2)}) async-start(), calls=%async_computation.6 | async-start | bytes 3112960 | tf_op jit(solution)/shard_map/all_gather | solution.py:24
  8.6 115.2 %reduce-scatter.3.cloned.1.call-start = ((), (), s32[]{:S(2)}) async-start(), calls=%async_computation.7 | async-start | bytes 3112960 | tf_op jit(solution)/shard_map/reduce_scatter | solution.py:30
  91.0 57.7 %copy-start.3 = (s32[256]{0:T(256)S(1)}, s32[256]{0:T(256)}, u32[]{:S(2)}) copy-start(s32[256]{0:T(256)} %param.10) | copy-start | bytes 3076
  91.0 67.5 %copy-start = (f32[64,2400]{1,0:T(8,128)S(1)}, f32[64,2400]{1,0:T(8,128)}, u32[]{:S(2)}) copy-start(f32[64,2400]{1,0:T(8,128)} %param.6) | copy-start | bytes 1843204
  91.0 67.5 %copy-start.1 = (f32[2400]{0:T(1024)S(1)}, f32[2400]{0:T(1024)}, u32[]{:S(2)}) copy-start(f32[2400]{0:T(1024)} %param.9) | copy-start | bytes 28804
  91.0 67.5 %copy-start.2 = (f32[64]{0:T(128)S(1)}, f32[64]{0:T(128)}, u32[]{:S(2)}) copy-start(f32[64]{0:T(128)} %param.8) | copy-start | bytes 772
  145.2 13.4 %all-to-all-start.1 = ((f32[16,4,2400]{2,0,1:T(8,128)}), f32[16,4,2400]{2,0,1:T(8,128)S(1)}, u32[]{:S(2)}, u32[]{:S(2)}) async-start(f32[16,4,2400]{2,0,1:T(8,128)} %bitcast.4), calls=%async_computation.2 | async-start | bytes 1245184 | tf_op jit(solution)/shard_map/all_to_all | solution.py:31
  148.7 61.9 %all-gather.5.cloned.1.call-start = ((), (), s32[]{:S(2)}) async-start(), calls=%async_computation.8 | async-start | bytes 3112960 | tf_op jit(solution)/shard_map/all_gather | solution.py:24
  159.6 110.5 %reduce-scatter.5.cloned.1.call-start = ((), (), s32[]{:S(2)}) async-start(), calls=%async_computation.9 | async-start | bytes 3112960 | tf_op jit(solution)/shard_map/reduce_scatter | solution.py:30
Sparse Core Ops, SparseCore 0:
  8.9 55.2 all-gather.2
  91.2 32.6 reduce-scatter.2
  159.7 50.7 all-gather.4
  237.4 32.6 reduce-scatter.4
where the time goes:
time: 312 us; the launch traced here: 311 us
  waiting for transfers between devices  181 us (58%)
  blocking collectives  54.8 us (18%)
  matrix products  53.5 us (17%)
  between operations  13.2 us (4%)
  other arithmetic  4.18 us (1%)
  starting transfers between devices  3.61 us (1%)
    all_gather x2, waiting for transfers between devices, per_device(): lax.all_gather(folded, 'con', axis=1, tiled=True)  106 us
    reduce_scatter x2, waiting for transfers between devices, per_device(): lax.psum_scatter(partial_value, ('rep', 'sub'), scatter_dimension=0, tile...  65.6 us
    dot_general x2, matrix products, per_device(): jnp.einsum('gmc,ac->gma', lax.all_gather(folded, 'con', axis=1, tiled=Tru...  53.5 us
    all_to_all x2, blocking collectives, per_device(): lax.all_to_all(reduced, 'con', split_axis=0, concat_axis=1, tiled=True)  42.5 us
    all_to_all x1, blocking collectives, per_device(): lax.all_to_all(lax.all_to_all(reduced, 'con', split_axis=0, concat_axis=1...  12.3 us
    all_to_all x1, waiting for transfers between devices, per_device(): lax.all_to_all(lax.all_to_all(reduced, 'con', split_axis=0, concat_axis=1...  8.93 us
  transfers between devices with their start and end apart: 5, of which 5 were waited for; matrix products, arithmetic and copies ran while one was open for 0% of the time, Pallas kernels for 0%

commit v1 on v0

v1 whole, which is shorter than its diff:
```python
import functools

import jax
import jax.numpy as jnp
from jax import lax
from jax.experimental import pallas as pl
from jax.experimental.pallas import tpu as pltpu
from jax.sharding import PartitionSpec as P

ITERS = 2
LABELS = 8
MESH = pl.DeviceIdType.MESH
VMEM = pl.BlockSpec(memory_space=pltpu.VMEM)
SMEM = pl.BlockSpec(memory_space=pltpu.SMEM)


class Dims:
    pass


def take_rows(ref, start, count, *window):
    shift = start % 8
    rows = ref[(*window[:-1], pl.ds(pl.multiple_of(start - shift, 8), count + 8), window[-1])]
    return pltpu.roll(rows, (count + 8 - shift) % (count + 8), 0)[:count]


def pack_kernel(d, tiles, x_ref, label_ref, energy_ref, out_ref, wide):
    for b in range(d.m):
        wide[:, (d.v // 128) * 128 :] = jnp.zeros_like(wide[:, (d.v // 128) * 128 :])
        wide[:, : d.v] = x_ref[:, b * d.v : (b + 1) * d.v]
        value = jnp.zeros((d.rows, d.w), jnp.float32)
        for label in range(LABELS):
            start = pl.multiple_of(tiles[2 + b, label] // 128 * 128, 128)
            value = jnp.where(label_ref[...] == label, wide[:, pl.ds(start, d.w)], value)
        lane = lax.broadcasted_iota(jnp.int32, (d.rows, d.w), 1)
        out_ref[b] = jnp.where(lane == d.w - 1, energy_ref[...], value)


def line_copies(z, n, view, up_send, up_recv, down_send, down_recv):
    def at(t):
        up_block = jnp.maximum(z - t, 0)
        down_block = jnp.minimum(z + t, n - 1)
        up = pltpu.make_async_remote_copy(
            src_ref=view(up_block),
            dst_ref=view(up_block),
            send_sem=up_send.at[t],
            recv_sem=up_recv.at[t],
            device_id={"con": jnp.minimum(z + 1, n - 1)},
            device_id_type=MESH,
        )
        down = pltpu.make_async_remote_copy(
            src_ref=view(down_block),
            dst_ref=view(down_block),
            send_sem=down_send.at[t],
            recv_sem=down_recv.at[t],
            device_id={"con": jnp.maximum(z - 1, 0)},
            device_id_type=MESH,
        )
        return up, down, (z >= t) & (z < n - 1), (z + t <= n - 1) & (z > 0)

    return at


def line_gather(z, n, view, sems, arrived):
    at = line_copies(z, n, view, *sems)
    for t in range(n - 1):
        up, down, can_up, can_down = at(t)
        pl.when(can_up)(up.start)
        pl.when(can_down)(down.start)

        @pl.when(z - 1 - t >= 0)
        def _():
            up.wait_recv()
            arrived(z - 1 - t)

        @pl.when(z + 1 + t <= n - 1)
        def _():
            down.wait_recv()
            arrived(z + 1 + t)

    for t in range(n - 1):
        up, down, can_up, can_down = at(t)
        pl.when(can_up)(up.wait_send)
        pl.when(can_down)(down.wait_send)


def greet(z, n, others):
    barrier = pltpu.get_barrier_semaphore()
    for other in others:
        pl.semaphore_signal(barrier, inc=1, device_id=other, device_id_type=MESH)

    @pl.when(z > 0)
    def _():
        pl.semaphore_signal(barrier, inc=1, device_id={"con": z - 1}, device_id_type=MESH)

    @pl.when(z < n - 1)
    def _():
        pl.semaphore_signal(barrier, inc=1, device_id={"con": z + 1}, device_id_type=MESH)

    near = (z > 0).astype(jnp.int32) + (z < n - 1).astype(jnp.int32)
    pl.semaphore_wait(barrier, near + len(others))


def gather_kernel(d, x_ref, out_ref, *sems):
    z = lax.axis_index("con")
    greet(z, d.con, [])

    def view(block):
        return out_ref.at[:, pl.ds(pl.multiple_of(block * d.rows, 8), d.rows), :]

    out_ref[:, pl.ds(pl.multiple_of(z * d.rows, 8), d.rows), :] = x_ref[...]
    line_gather(z, d.con, view, sems, lambda block: None)


def reduce_kernel(d, x_ref, out_ref, landed, whole, s_send, s_recv, x_send, x_recv, *sems):
    z = lax.axis_index("con")
    j = lax.axis_index("rep") * d.sub + lax.axis_index("sub")

    def device(q):
        return {"rep": q // d.sub, "sub": q % d.sub}

    greet(z, d.con, [device((j + k) % d.rs) for k in range(1, d.rs)])
    copies = []
    for k in range(1, d.rs):
        q = (j + k) % d.rs
        copy = pltpu.make_async_remote_copy(
            src_ref=x_ref.at[q],
            dst_ref=landed.at[k - 1],
            send_sem=s_send.at[k - 1],
            recv_sem=s_recv.at[k - 1],
            device_id=device(q),
            device_id_type=MESH,
        )
        copy.start()
        copies.append(copy)
    total = x_ref[j]
    for k in range(1, d.rs):
        copies[k - 1].wait_recv()
        total = total + landed[k - 1]
    whole[z] = total

    def to_owner(block):
        owner = block // d.m
        return owner, pltpu.make_async_remote_copy(
            src_ref=whole.at[block],
            dst_ref=out_ref.at[block % d.m, j],
            send_sem=x_send.at[block],
            recv_sem=x_recv.at[block % d.m, j],
            device_id=device(owner),
            device_id_type=MESH,
        )

    def arrived(block):
        owner, copy = to_owner(block)
        pl.when(owner != j)(copy.start)

        @pl.when(owner == j)
        def _():
            out_ref[block % d.m, j] = whole[block]

    arrived(z)
    line_gather(z, d.con, lambda block: whole.at[block], sems, arrived)
    for block in range(d.con):
        owner, copy = to_owner(block)
        pl.when(owner != j)(copy.wait_send)
    for b in range(d.m):
        for k in range(1, d.rs):
            q = (j + k) % d.rs
            pltpu.make_async_remote_copy(
                src_ref=whole.at[0],
                dst_ref=out_ref.at[b, q],
                send_sem=x_send.at[0],
                recv_sem=x_recv.at[b, q],
                device_id=device(q),
                device_id_type=MESH,
            ).wait_recv()
    for copy in copies:
        copy.wait_send()


def product(d, info, label_ref, ladder_ref, out_ref, high_low, low, high):
    step = pl.program_id(0)
    row = lax.broadcasted_iota(jnp.int32, (d.cw, d.cols), 0) + step * d.cw
    value = jnp.where((row >= low[...]) & (row < high[...]), ladder_ref[...], 0.0)
    value_high = value.astype(jnp.bfloat16)
    value_low = (value - value_high.astype(jnp.float32)).astype(jnp.bfloat16)
    dims = (((1,), (1,)), ((), ()))
    first = lax.dot_general(value_high, high_low[...], dims, preferred_element_type=jnp.float32)
    second = lax.dot_general(
        value_low, high_low[: d.s, :], dims, preferred_element_type=jnp.float32
    )
    out_ref[0] = jnp.transpose(first[:, : d.s] + first[:, d.s :] + second)


def prepare(d, info, label_ref, amp, high_low, low, high):
    value = amp[...]
    value_high = value.astype(jnp.bfloat16)
    high_low[: d.s, :] = value_high
    high_low[d.s :, :] = (value - value_high.astype(jnp.float32)).astype(jnp.bfloat16)
    first = jnp.zeros((1, d.cols), jnp.int32)
    last = jnp.zeros((1, d.cols), jnp.int32)
    for label in range(LABELS):
        here = label_ref[...] == label
        first = jnp.where(here, info[2 + d.m, label], first)
        last = jnp.where(here, info[3 + d.m, label], last)
    low[...] = first
    high[...] = last


def first_kernel(
    d, info, got_ref, wide_label, wide_energy, label_ref, ladder_ref,
    out_ref, ints_ref, div_ref, amp, high_low, low, high,
):
    @pl.when(pl.program_id(0) == 0)
    def _():
        ints_ref[...] = jnp.zeros_like(ints_ref)
        div_ref[...] = jnp.ones_like(div_ref)
        slot = lax.broadcasted_iota(jnp.int32, (d.s, d.w), 0)
        for b in range(d.m):
            for label in range(LABELS):
                start = pl.multiple_of(info[2 + b, label] // 128 * 128, 128)
                rows = take_rows(got_ref, info[0, label], d.s, b, slice(None))
                window = pl.ds(start, d.w)
                good = (wide_label[b, :, window] == label) & (slot < info[1, label])
                divisor = wide_energy[b, :, window] - rows[:, d.w - 1 : d.w]
                ints_ref[b, :, window] = jnp.where(good, rows, ints_ref[b, :, window])
                div_ref[b, :, window] = jnp.where(good, divisor, div_ref[b, :, window])
            amp[:, b * d.v : (b + 1) * d.v] = ints_ref[b, :, : d.v] / div_ref[b, :, : d.v]
        prepare(d, info, label_ref, amp, high_low, low, high)

    product(d, info, label_ref, ladder_ref, out_ref, high_low, low, high)


def update(d, b, sum_ref, ints_ref, div_ref):
    term = jnp.concatenate([sum_ref[b, q] for q in range(d.rs)], axis=1)
    return (ints_ref[b, :, : d.vp] + term) / div_ref[b, :, : d.vp]


def next_kernel(
    d, info, sum_ref, ints_ref, div_ref, label_ref, ladder_ref, out_ref, amp, high_low, low, high
):
    @pl.when(pl.program_id(0) == 0)
    def _():
        for b in range(d.m):
            amp[:, b * d.v : (b + 1) * d.v] = update(d, b, sum_ref, ints_ref, div_ref)[:, : d.v]
        prepare(d, info, label_ref, amp, high_low, low, high)

    product(d, info, label_ref, ladder_ref, out_ref, high_low, low, high)


def final_kernel(d, info, sum_ref, ints_ref, div_ref, wide_label, row_label, out_ref, slots, wide):
    base = lax.axis_index("con") * d.rows
    for b in range(d.m):
        slots[...] = jnp.zeros_like(slots)
        slots[d.rows : d.rows + d.s, : d.vp] = update(d, b, sum_ref, ints_ref, div_ref)
        wide[...] = jnp.zeros_like(wide)
        for label in range(LABELS):
            start = pl.multiple_of(info[2 + b, label] // 128 * 128, 128)
            window = pl.ds(start, d.w)
            place = jnp.clip(base - info[0, label] + d.rows, 0, d.rows + d.s)
            rows = take_rows(slots, place, d.rows, window)
            good = (wide_label[b, :, window] == label) & (row_label[...] == label)
            wide[:, window] = jnp.where(good, rows, wide[:, window])
        out_ref[:, b * d.v : (b + 1) * d.v] = wide[:, : d.v]


def per_device(integrals, ladder, pair_energy, virt_energy, pair_irrep, virt_irrep):
    d = Dims()
    d.con = lax.axis_size("con")
    d.sub = lax.axis_size("sub")
    d.rs = lax.axis_size("rep") * d.sub
    d.rows, d.cols = integrals.shape
    d.v = ladder.shape[0]
    d.m = d.cols // d.v
    d.s = pair_irrep.shape[0] * 3 // 16
    tiles = pl.cdiv(d.v, 128)
    d.w = 128 * pl.cdiv(d.v // 4 + 128, 128)
    d.cw = 128 * pl.cdiv(tiles, d.rs)
    d.vp = d.cw * d.rs
    d.pw = max(d.vp, 128 * (tiles - 1) + d.w)
    con_index = lax.axis_index("con")
    rs_index = lax.axis_index(("rep", "sub"))
    f32 = jnp.float32
    i32 = jnp.int32

    labels = jnp.arange(LABELS, dtype=i32)

    def below(values, upto):
        return jnp.sum((values[None, :] < upto[:, None]).astype(i32), axis=1)

    virt_local = lax.dynamic_slice_in_dim(virt_irrep, rs_index * d.cols, d.cols)
    virt_own = lax.dynamic_slice_in_dim(virt_irrep, con_index * d.v, d.v)
    row_label = lax.dynamic_slice_in_dim(pair_irrep, con_index * d.rows, d.rows)[:, None]
    row_start = below(pair_irrep, labels)
    row_count = below(pair_irrep, labels + 1) - row_start
    blocks = virt_local.reshape(d.m, d.v)
    info = jnp.stack(
        [row_start, row_count]
        + [below(blocks[b], labels) for b in range(d.m)]
        + [below(virt_own, labels), below(virt_own, labels + 1)]
    )
    info = jnp.minimum(info, jnp.where(jnp.arange(d.m + 4)[:, None] < 2, 1 << 20, d.v))
    info = info.at[2 : 2 + d.m].min(d.v - 1)
    pad = ((0, 0), (0, d.pw - d.v))
    wide_label = jnp.pad(blocks, pad, constant_values=-1)[:, None, :]
    wide_energy = jnp.pad(virt_energy.reshape(d.m, d.v), pad)[:, None, :]
    col_label = virt_local[None, :]

    limit = pltpu.CompilerParams(vmem_limit_bytes=48 * 1024 * 1024)
    packed = pl.pallas_call(
        functools.partial(pack_kernel, d),
        out_shape=jax.ShapeDtypeStruct((d.m, d.rows, d.w), f32),
        in_specs=[SMEM, VMEM, VMEM, VMEM],
        out_specs=VMEM,
        scratch_shapes=[pltpu.VMEM((d.rows, d.pw), f32)],
        compiler_params=limit,
    )(info, integrals, row_label, pair_energy[:, None])

    line_sems = [pltpu.SemaphoreType.DMA((d.con - 1,))] * 4
    got = pl.pallas_call(
        functools.partial(gather_kernel, d),
        out_shape=jax.ShapeDtypeStruct((d.m, d.con * d.rows + d.s + 8, d.w), f32),
        in_specs=[VMEM],
        out_specs=VMEM,
        scratch_shapes=line_sems,
        compiler_params=pltpu.CompilerParams(
            collective_id=0, has_side_effects=True, vmem_limit_bytes=32 * 1024 * 1024
        ),
    )(packed)

    piece = (d.rs, d.s, d.cw)
    last_block = pl.cdiv(d.v, d.cw) - 1
    ladder_spec = pl.BlockSpec((d.cw, d.cols), lambda i: (jnp.minimum(i, last_block), 0))
    out_spec = pl.BlockSpec((1, d.s, d.cw), lambda i: (i, 0, 0))
    keep = [
        pltpu.VMEM((d.s, d.cols), f32),
        pltpu.VMEM((2 * d.s, d.cols), jnp.bfloat16),
        pltpu.VMEM((1, d.cols), i32),
        pltpu.VMEM((1, d.cols), i32),
    ]
    slot = jax.ShapeDtypeStruct((d.m, d.s, d.pw), f32)
    part, ints, divisor = pl.pallas_call(
        functools.partial(first_kernel, d),
        grid=(d.rs,),
        out_shape=(jax.ShapeDtypeStruct(piece, f32), slot, slot),
        in_specs=[SMEM, VMEM, VMEM, VMEM, VMEM, ladder_spec],
        out_specs=(out_spec, VMEM, VMEM),
        scratch_shapes=keep,
        compiler_params=limit,
    )(info, got, wide_label, wide_energy, col_label, ladder)

    for repeat in range(ITERS):
        if repeat > 0:
            part = pl.pallas_call(
                functools.partial(next_kernel, d),
                grid=(d.rs,),
                out_shape=jax.ShapeDtypeStruct(piece, f32),
                in_specs=[SMEM, VMEM, VMEM, VMEM, VMEM, ladder_spec],
                out_specs=out_spec,
                scratch_shapes=keep,
                compiler_params=limit,
            )(info, summed, ints, divisor, col_label, ladder)
        summed = pl.pallas_call(
            functools.partial(reduce_kernel, d),
            out_shape=jax.ShapeDtypeStruct((d.m,) + piece, f32),
            in_specs=[VMEM],
            out_specs=VMEM,
            scratch_shapes=[
                pltpu.VMEM((d.rs - 1, d.s, d.cw), f32),
                pltpu.VMEM((d.con, d.s, d.cw), f32),
                pltpu.SemaphoreType.DMA((d.rs - 1,)),
                pltpu.SemaphoreType.DMA((d.rs - 1,)),
                pltpu.SemaphoreType.DMA((d.con,)),
                pltpu.SemaphoreType.DMA((d.m, d.rs)),
            ]
            + line_sems,
            compiler_params=pltpu.CompilerParams(
                collective_id=1 + repeat, has_side_effects=True, vmem_limit_bytes=32 * 1024 * 1024
            ),
        )(part)

    return pl.pallas_call(
        functools.partial(final_kernel, d),
        out_shape=jax.ShapeDtypeStruct((d.rows, d.cols), f32),
        in_specs=[SMEM, VMEM, VMEM, VMEM, VMEM, VMEM],
        out_specs=VMEM,
        scratch_shapes=[
            pltpu.VMEM((2 * d.rows + d.s + 8, d.pw), f32),
            pltpu.VMEM((d.rows, d.pw), f32),
        ],
        compiler_params=limit,
    )(info, summed, ints, divisor, wide_label, row_label)


def solution(mesh):
    in_specs = (
        P(("grp", "con"), ("rep", "sub")),
        P(("grp", "con"), ("rep", "sub")),
        P(("grp", "con")),
        P(("grp", "rep", "sub")),
        P("grp"),
        P("grp"),
    )
    out_specs = P(("grp", "con"), ("rep", "sub"))
    return jax.shard_map(
        per_device, mesh=mesh, in_specs=in_specs, out_specs=out_specs, check_vma=False
    )
```

time: 312 us -> 103 us (0.33)
  waiting for transfers between devices: 181 us -> 0 us
  Pallas kernels: 0 us -> 97.3 us
  blocking collectives: 54.8 us -> 0 us
  matrix products: 53.5 us -> 0 us
  between operations: 13.2 us -> 0.07 us
  starting transfers between devices: 3.61 us -> 0 us
  local copies, waits for them, and re-layouts: 0.89 us -> 4.34 us
    all_gather x2 -> x0, waiting for transfers between devices: 106 us -> none  [per_device(): lax.all_gather(folded, 'con', axis=1, tiled=True)]
    pallas_call x0 -> x7, Pallas kernels: none -> 97.3 us  [the longest x2 47.9 us: per_device(): pl.pallas_call(functools.partial(reduce_kernel, d), out_shape=jax.ShapeDt...]
    reduce_scatter x2 -> x0, waiting for transfers between devices: 65.6 us -> none  [per_device(): lax.psum_scatter(partial_value, ('rep', 'sub'), scatter_dimension=0, tile...]
    all_to_all x3 -> x0, blocking collectives: 54.8 us -> none  [the longest x2 42.5 us: per_device(): lax.all_to_all(reduced, 'con', split_axis=0, concat_axis=1, tiled=True)]
    dot_general x2 -> x0, matrix products: 53.5 us -> none  [per_device(): jnp.einsum('gmc,ac->gma', lax.all_gather(folded, 'con', axis=1, tiled=Tru...]
    all_to_all x1 -> x0, waiting for transfers between devices: 8.93 us -> none  [per_device(): lax.all_to_all(lax.all_to_all(reduced, 'con', split_axis=0, concat_axis=1...]
    div x3 -> x0, other arithmetic: 4.18 us -> none  [the longest x2 2.1 us: per_device(): (integrals + jnp.where(allowed, ladder_term, jnp.zeros_like(ladder_term))...]
    all_to_all x1 -> x0, starting transfers between devices: 3.48 us -> none  [per_device(): lax.all_to_all(lax.all_to_all(reduced, 'con', split_axis=0, concat_axis=1...]
  transfers between devices with their start and end apart: 5 -> 0, of which waited for: 5 -> 0; matrix products, arithmetic and copies ran while one was open for 0% -> 0% of each run, Pallas kernels for 0% -> 0%
where the time goes in v1:
time: 103 us
  Pallas kernels  97.3 us (94%)
  local copies, waits for them, and re-layouts  4.34 us (4%)
  other arithmetic  1.18 us (1%)
    pallas_call x2, Pallas kernels, per_device(): pl.pallas_call(functools.partial(reduce_kernel, d), out_shape=jax.ShapeDt...  47.9 us
    pallas_call x1, Pallas kernels, per_device(): pl.pallas_call(functools.partial(gather_kernel, d), out_shape=jax.ShapeDt...  19.2 us
    pallas_call x1, Pallas kernels, per_device(): pl.pallas_call(functools.partial(first_kernel, d), grid=(d.rs,), out_shap...  14 us
    pallas_call x1, Pallas kernels, per_device(): pl.pallas_call(functools.partial(next_kernel, d), grid=(d.rs,), out_shape...  13.2 us
    pallas_call x1, Pallas kernels, per_device(): pl.pallas_call(functools.partial(final_kernel, d), out_shape=jax.ShapeDty...  2.23 us

profile of v1, /device:TPU:0, one launch (start us, length us, event | category | flops | bytes accessed | tf_op | source)
XLA Modules:
  0.0 102.8 jit_solution(15612668346273509775)
XLA Ops:
  0.0 0.8 dynamic-slice_bitcast_fusion
  0.8 0.9 convert_reduce_fusion.3
  1.7 0.7 reshape.53
  2.4 0.9 fusion
  3.3 0.2 convert_reduce_fusion
  3.5 0.1 broadcast_minimum_fusion
  3.6 0.1 copy.10.label_ref.row_label
  3.7 0.7 copy.11.energy_ref
  4.5 0.0 copy-start
  4.5 1.1 %copy-done = f32[64,2400]{1,0:T(8,128)S(1)} copy-done((f32[64,2400]{1,0:T(8,128)S(1)}, f32[64,2400]{1,0:T(8,128)}, u32[]{:S(2)}) %copy-start) | copy-done | bytes 614424
  5.5 0.8 shard_map.64.x_ref
  6.3 19.2 %shard_map.65.got_ref = f32[1,312,768]{2,1,0:T(8,128)S(1)} custom-call(f32[1,64,768]{2,1,0:T(8,128)S(1)} %shard_map.64.x_ref), custom_call_target="tpu_custom_call" | custom-call | tf_op jit(solution)/shard_map/pallas_call | solution.py:320
  25.5 14.0 %shard_map.66 = (f32[4,48,640]{2,1,0:T(8,128)S(1)}, f32[1,48,3072]{2,1,0:T(8,128)S(1)}, f32[1,48,3072]{2,1,0:T(8,128)S(1)}) custom-call(s32[5,8]{1,0:T(8,128)S(1)} %scatter-min.4.tiles.info, f32[1,312,768]{2,1,0:T(8,128)S(1)} %shard_map.65.got_ref, s32[1,1,3072]{2,1,0:T(1,128)S(1)} %pad_bitcast_fusion.1.wide_label, ...), custom_call_target="tpu_custom_call" | custom-call | tf_op jit(solution)/shard_map/pallas_call | solution.py:342
  39.5 23.5 %shard_map.67.sum_ref = f32[1,4,48,640]{3,2,1,0:T(8,128)S(1)} custom-call(f32[4,48,640]{2,1,0:T(8,128)S(1)} %get-tuple-element.20.x_ref), custom_call_target="tpu_custom_call" | custom-call | tf_op jit(solution)/shard_map/pallas_call | solution.py:363
  63.0 13.2 %shard_map.68.x_ref = f32[4,48,640]{2,1,0:T(8,128)S(1)} custom-call(s32[5,8]{1,0:T(8,128)S(1)} %scatter-min.4.tiles.info, f32[1,4,48,640]{3,2,1,0:T(8,128)S(1)} %shard_map.67.sum_ref, f32[1,48,3072]{2,1,0:T(8,128)S(1)} %get-tuple-element.21.ints_ref, f32[1,48,3072]{2,1,0:T(8,128)S(1)} %get-tuple-element.22.div_ref, ...), custom_call_target="tpu_custom_call" | custom-call | tf_op jit(solution)/shard_map/pallas_call | solution.py:354
  76.2 24.4 %shard_map.69.sum_ref = f32[1,4,48,640]{3,2,1,0:T(8,128)S(1)} custom-call(f32[4,48,640]{2,1,0:T(8,128)S(1)} %shard_map.68.x_ref), custom_call_target="tpu_custom_call" | custom-call | tf_op jit(solution)/shard_map/pallas_call | solution.py:363
  100.6 2.2 %shard_map.70 = f32[64,2400]{1,0:T(8,128)} custom-call(s32[5,8]{1,0:T(8,128)S(1)} %scatter-min.4.tiles.info, f32[1,4,48,640]{3,2,1,0:T(8,128)S(1)} %shard_map.69.sum_ref, f32[1,48,3072]{2,1,0:T(8,128)S(1)} %get-tuple-element.21.ints_ref, f32[1,48,3072]{2,1,0:T(8,128)S(1)} %get-tuple-element.22.div_ref, s32[1,1,3072]{2,1,0:T(1,128)S(1)} %pad_bitcast_fusion.1.wide_label, ...), custom_call_target="tpu_custom_call" | custom-call | tf_op jit(solution)/shard_map/pallas_call | solution.py:382
  (9 shorter events, 0.1 us)
Async XLA Ops:
  4.5 1.1 %copy-start = (f32[64,2400]{1,0:T(8,128)S(1)}, f32[64,2400]{1,0:T(8,128)}, u32[]{:S(2)}) copy-start(f32[64,2400]{1,0:T(8,128)} %x_ref.1) | copy-start | bytes 1843204

commit v2 on v1

--- a/solution.py
+++ b/solution.py
@@ -9,6 +9,8 @@
 
 ITERS = 2
 LABELS = 8
+PARTS = 2
+CHUNK = 256
 MESH = pl.DeviceIdType.MESH
 VMEM = pl.BlockSpec(memory_space=pltpu.VMEM)
 SMEM = pl.BlockSpec(memory_space=pltpu.SMEM)
@@ -30,8 +32,10 @@
         wide[:, : d.v] = x_ref[:, b * d.v : (b + 1) * d.v]
         value = jnp.zeros((d.rows, d.w), jnp.float32)
         for label in range(LABELS):
-            start = pl.multiple_of(tiles[2 + b, label] // 128 * 128, 128)
-            value = jnp.where(label_ref[...] == label, wide[:, pl.ds(start, d.w)], value)
+            shift = tiles[2 + b, label] % 128
+            start = pl.multiple_of(tiles[2 + b, label] - shift, 128)
+            window = pltpu.roll(wide[:, pl.ds(start, d.w + 128)], d.w + 128 - shift, 1)
+            value = jnp.where(label_ref[...] == label, window[:, : d.w], value)
         lane = lax.broadcasted_iota(jnp.int32, (d.rows, d.w), 1)
         out_ref[b] = jnp.where(lane == d.w - 1, energy_ref[...], value)
 
@@ -61,27 +65,42 @@
     return at
 
 
-def line_gather(z, n, view, sems, arrived):
-    at = line_copies(z, n, view, *sems)
-    for t in range(n - 1):
-        up, down, can_up, can_down = at(t)
+def line_gather(z, n, view, sems, ready, arrived):
+    at = [
+        line_copies(z, n, functools.partial(view, h), *[sem.at[h] for sem in sems])
+        for h in range(PARTS)
+    ]
+
+    def send(h, t):
+        up, down, can_up, can_down = at[h](t)
         pl.when(can_up)(up.start)
         pl.when(can_down)(down.start)
 
-        @pl.when(z - 1 - t >= 0)
-        def _():
-            up.wait_recv()
-            arrived(z - 1 - t)
-
-        @pl.when(z + 1 + t <= n - 1)
-        def _():
-            down.wait_recv()
-            arrived(z + 1 + t)
-
+    for h in range(PARTS):
+        ready(h)
+        send(h, 0)
+        arrived(h, z)
     for t in range(n - 1):
-        up, down, can_up, can_down = at(t)
-        pl.when(can_up)(up.wait_send)
-        pl.when(can_down)(down.wait_send)
+        for h in range(PARTS):
+            up, down, _, _ = at[h](t)
+            pl.when(z - 1 - t >= 0)(up.wait_recv)
+            pl.when(z + 1 + t <= n - 1)(down.wait_recv)
+            if t + 1 < n - 1:
+                send(h, t + 1)
+
+            @pl.when(z - 1 - t >= 0)
+            def _():
+                arrived(h, z - 1 - t)
+
+            @pl.when(z + 1 + t <= n - 1)
+            def _():
+                arrived(h, z + 1 + t)
+
+    for t in range(n - 1):
+        for h in range(PARTS):
+            up, down, can_up, can_down = at[h](t)
+            pl.when(can_up)(up.wait_send)
+            pl.when(can_down)(down.wait_send)
 
 
 def greet(z, n, others):
@@ -105,11 +124,13 @@
     z = lax.axis_index("con")
     greet(z, d.con, [])
 
-    def view(block):
-        return out_ref.at[:, pl.ds(pl.multiple_of(block * d.rows, 8), d.rows), :]
+    rows = d.rows // PARTS
+
+    def view(h, block):
+        return out_ref.at[:, pl.ds(pl.multiple_of(block * d.rows + h * rows, 8), rows), :]
 
     out_ref[:, pl.ds(pl.multiple_of(z * d.rows, 8), d.rows), :] = x_ref[...]
-    line_gather(z, d.con, view, sems, lambda block: None)
+    line_gather(z, d.con, view, sems, lambda h: None, lambda h, block: None)
 
 
 def reduce_kernel(d, x_ref, out_ref, landed, whole, s_send, s_recv, x_send, x_recv, *sems):
@@ -120,76 +141,96 @@
         return {"rep": q // d.sub, "sub": q % d.sub}
 
     greet(z, d.con, [device((j + k) % d.rs) for k in range(1, d.rs)])
+    rows = d.s // PARTS
+    part = [pl.ds(h * rows, rows) for h in range(PARTS)]
     copies = []
-    for k in range(1, d.rs):
-        q = (j + k) % d.rs
-        copy = pltpu.make_async_remote_copy(
-            src_ref=x_ref.at[q],
-            dst_ref=landed.at[k - 1],
-            send_sem=s_send.at[k - 1],
-            recv_sem=s_recv.at[k - 1],
-            device_id=device(q),
-            device_id_type=MESH,
-        )
-        copy.start()
-        copies.append(copy)
-    total = x_ref[j]
-    for k in range(1, d.rs):
-        copies[k - 1].wait_recv()
-        total = total + landed[k - 1]
-    whole[z] = total
-
-    def to_owner(block):
+    for h in range(PARTS):
+        for k in range(1, d.rs):
+            q = (j + k) % d.rs
+            copy = pltpu.make_async_remote_copy(
+                src_ref=x_ref.at[q, part[h]],
+                dst_ref=landed.at[k - 1, part[h]],
+                send_sem=s_send.at[h, k - 1],
+                recv_sem=s_recv.at[h, k - 1],
+                device_id=device(q),
+                device_id_type=MESH,
+            )
+            copy.start()
+            copies.append(copy)
+
+    def ready(h):
+        total = x_ref[j, part[h]]
+        for k in range(1, d.rs):
+            copies[h * (d.rs - 1) + k - 1].wait_recv()
+            total = total + landed[k - 1, part[h]]
+        whole[z, part[h]] = total
+
+    def to_owner(h, block):
         owner = block // d.m
         return owner, pltpu.make_async_remote_copy(
-            src_ref=whole.at[block],
-            dst_ref=out_ref.at[block % d.m, j],
-            send_sem=x_send.at[block],
-            recv_sem=x_recv.at[block % d.m, j],
+            src_ref=whole.at[block, part[h]],
+            dst_ref=out_ref.at[block % d.m, j, part[h]],
+            send_sem=x_send.at[h, block],
+            recv_sem=x_recv.at[h, block % d.m, j],
             device_id=device(owner),
             device_id_type=MESH,
         )
 
-    def arrived(block):
-        owner, copy = to_owner(block)
+    def arrived(h, block):
+        owner, copy = to_owner(h, block)
         pl.when(owner != j)(copy.start)
 
         @pl.when(owner == j)
         def _():
-            out_ref[block % d.m, j] = whole[block]
-
-    arrived(z)
-    line_gather(z, d.con, lambda block: whole.at[block], sems, arrived)
-    for block in range(d.con):
-        owner, copy = to_owner(block)
-        pl.when(owner != j)(copy.wait_send)
-    for b in range(d.m):
-        for k in range(1, d.rs):
-            q = (j + k) % d.rs
-            pltpu.make_async_remote_copy(
-                src_ref=whole.at[0],
-                dst_ref=out_ref.at[b, q],
-                send_sem=x_send.at[0],
-                recv_sem=x_recv.at[b, q],
-                device_id=device(q),
-                device_id_type=MESH,
-            ).wait_recv()
+            out_ref[block % d.m, j, part[h]] = whole[block, part[h]]
+
+    line_gather(z, d.con, lambda h, block: whole.at[block, part[h]], sems, ready, arrived)
+    for h in range(PARTS):
+        for block in range(d.con):
+            owner, copy = to_owner(h, block)
+            pl.when(owner != j)(copy.wait_send)
+        for b in range(d.m):
+            for k in range(1, d.rs):
+                q = (j + k) % d.rs
+                pltpu.make_async_remote_copy(
+                    src_ref=whole.at[0, part[h]],
+                    dst_ref=out_ref.at[b, q, part[h]],
+                    send_sem=x_send.at[h, 0],
+                    recv_sem=x_recv.at[h, b, q],
+                    device_id=device(q),
+                    device_id_type=MESH,
+                ).wait_recv()
     for copy in copies:
         copy.wait_send()
 
 
-def product(d, info, label_ref, ladder_ref, out_ref, high_low, low, high):
+def product(d, spans, ladder_ref, out_ref, high_low, low, high, acc):
     step = pl.program_id(0)
-    row = lax.broadcasted_iota(jnp.int32, (d.cw, d.cols), 0) + step * d.cw
-    value = jnp.where((row >= low[...]) & (row < high[...]), ladder_ref[...], 0.0)
-    value_high = value.astype(jnp.bfloat16)
-    value_low = (value - value_high.astype(jnp.float32)).astype(jnp.bfloat16)
     dims = (((1,), (1,)), ((), ()))
-    first = lax.dot_general(value_high, high_low[...], dims, preferred_element_type=jnp.float32)
-    second = lax.dot_general(
-        value_low, high_low[: d.s, :], dims, preferred_element_type=jnp.float32
-    )
-    out_ref[0] = jnp.transpose(first[:, : d.s] + first[:, d.s :] + second)
+    acc[...] = jnp.zeros_like(acc)
+    for half in range(2):
+        mine = d.chunks + step * 2 + half
+        here = pl.ds(half * d.half, d.half)
+        for chunk in range(d.chunks):
+            cut = slice(chunk * CHUNK, min((chunk + 1) * CHUNK, d.cols))
+
+            @pl.when((spans[0, mine] <= spans[1, chunk]) & (spans[0, chunk] <= spans[1, mine]))
+            def _():
+                row = lax.broadcasted_iota(jnp.int32, (d.half, cut.stop - cut.start), 0)
+                row = row + (step * d.cw + half * d.half)
+                keep = (row >= low[:, cut]) & (row < high[:, cut])
+                value = jnp.where(keep, ladder_ref[here, cut], 0.0)
+                value_high = value.astype(jnp.bfloat16)
+                value_low = (value - value_high.astype(jnp.float32)).astype(jnp.bfloat16)
+                first = lax.dot_general(
+                    value_high, high_low[:, cut], dims, preferred_element_type=jnp.float32
+                )
+                second = lax.dot_general(
+                    value_low, high_low[: d.s, cut], dims, preferred_element_type=jnp.float32
+                )
+                acc[here, :] += first[:, : d.s] + first[:, d.s :] + second
+
+    out_ref[0] = jnp.transpose(acc[...])
 
 
 def prepare(d, info, label_ref, amp, high_low, low, high):
@@ -208,27 +249,31 @@
 
 
 def first_kernel(
-    d, info, got_ref, wide_label, wide_energy, label_ref, ladder_ref,
-    out_ref, ints_ref, div_ref, amp, high_low, low, high,
+    d, info, spans, got_ref, wide_label, wide_energy, label_ref, ladder_ref,
+    out_ref, ints_ref, div_ref, amp, high_low, low, high, acc,
 ):
     @pl.when(pl.program_id(0) == 0)
     def _():
         ints_ref[...] = jnp.zeros_like(ints_ref)
         div_ref[...] = jnp.ones_like(div_ref)
-        slot = lax.broadcasted_iota(jnp.int32, (d.s, d.w), 0)
+        slot = lax.broadcasted_iota(jnp.int32, (d.s, d.w + 128), 0)
         for b in range(d.m):
             for label in range(LABELS):
-                start = pl.multiple_of(info[2 + b, label] // 128 * 128, 128)
+                shift = info[2 + b, label] % 128
+                start = pl.multiple_of(info[2 + b, label] - shift, 128)
                 rows = take_rows(got_ref, info[0, label], d.s, b, slice(None))
-                window = pl.ds(start, d.w)
+                energy = rows[:, d.w - 1 : d.w]
+                rows = jnp.concatenate([rows, jnp.zeros((d.s, 128), jnp.float32)], axis=1)
+                rows = pltpu.roll(rows, shift, 1)
+                window = pl.ds(start, d.w + 128)
                 good = (wide_label[b, :, window] == label) & (slot < info[1, label])
-                divisor = wide_energy[b, :, window] - rows[:, d.w - 1 : d.w]
+                divisor = wide_energy[b, :, window] - energy
                 ints_ref[b, :, window] = jnp.where(good, rows, ints_ref[b, :, window])
                 div_ref[b, :, window] = jnp.where(good, divisor, div_ref[b, :, window])
             amp[:, b * d.v : (b + 1) * d.v] = ints_ref[b, :, : d.v] / div_ref[b, :, : d.v]
         prepare(d, info, label_ref, amp, high_low, low, high)
 
-    product(d, info, label_ref, ladder_ref, out_ref, high_low, low, high)
+    product(d, spans, ladder_ref, out_ref, high_low, low, high, acc)
 
 
 def update(d, b, sum_ref, ints_ref, div_ref):
@@ -237,7 +282,8 @@
 
 
 def next_kernel(
-    d, info, sum_ref, ints_ref, div_ref, label_ref, ladder_ref, out_ref, amp, high_low, low, high
+    d, info, spans, sum_ref, ints_ref, div_ref, label_ref, ladder_ref,
+    out_ref, amp, high_low, low, high, acc,
 ):
     @pl.when(pl.program_id(0) == 0)
     def _():
@@ -245,7 +291,7 @@
             amp[:, b * d.v : (b + 1) * d.v] = update(d, b, sum_ref, ints_ref, div_ref)[:, : d.v]
         prepare(d, info, label_ref, amp, high_low, low, high)
 
-    product(d, info, label_ref, ladder_ref, out_ref, high_low, low, high)
+    product(d, spans, ladder_ref, out_ref, high_low, low, high, acc)
 
 
 def final_kernel(d, info, sum_ref, ints_ref, div_ref, wide_label, row_label, out_ref, slots, wide):
@@ -256,7 +302,7 @@
         wide[...] = jnp.zeros_like(wide)
         for label in range(LABELS):
             start = pl.multiple_of(info[2 + b, label] // 128 * 128, 128)
-            window = pl.ds(start, d.w)
+            window = pl.ds(start, d.w + 128)
             place = jnp.clip(base - info[0, label] + d.rows, 0, d.rows + d.s)
             rows = take_rows(slots, place, d.rows, window)
             good = (wide_label[b, :, window] == label) & (row_label[...] == label)
@@ -274,10 +320,10 @@
     d.m = d.cols // d.v
     d.s = pair_irrep.shape[0] * 3 // 16
     tiles = pl.cdiv(d.v, 128)
-    d.w = 128 * pl.cdiv(d.v // 4 + 128, 128)
+    d.w = 128 * pl.cdiv(d.v // 4 + 1, 128)
     d.cw = 128 * pl.cdiv(tiles, d.rs)
     d.vp = d.cw * d.rs
-    d.pw = max(d.vp, 128 * (tiles - 1) + d.w)
+    d.pw = max(d.vp, 128 * tiles + d.w)
     con_index = lax.axis_index("con")
     rs_index = lax.axis_index(("rep", "sub"))
     f32 = jnp.float32
@@ -301,6 +347,20 @@
     )
     info = jnp.minimum(info, jnp.where(jnp.arange(d.m + 4)[:, None] < 2, 1 << 20, d.v))
     info = info.at[2 : 2 + d.m].min(d.v - 1)
+    d.half = d.cw // 2
+    d.chunks = pl.cdiv(d.cols, CHUNK)
+
+    def cuts(values, count, size):
+        return jnp.pad(values, (0, count * size - values.shape[0]), mode="edge").reshape(count, size)
+
+    by_chunk = cuts(virt_local, d.chunks, CHUNK)
+    by_half = cuts(virt_own, 2 * d.rs, d.half)
+    spans = jnp.stack(
+        [
+            jnp.concatenate([by_chunk.min(axis=1), by_half.min(axis=1)]),
+            jnp.concatenate([by_chunk.max(axis=1), by_half.max(axis=1)]),
+        ]
+    )
     pad = ((0, 0), (0, d.pw - d.v))
     wide_label = jnp.pad(blocks, pad, constant_values=-1)[:, None, :]
     wide_energy = jnp.pad(virt_energy.reshape(d.m, d.v), pad)[:, None, :]
@@ -316,7 +376,7 @@
         compiler_params=limit,
     )(info, integrals, row_label, pair_energy[:, None])
 
-    line_sems = [pltpu.SemaphoreType.DMA((d.con - 1,))] * 4
+    line_sems = [pltpu.SemaphoreType.DMA((PARTS, d.con - 1))] * 4
     got = pl.pallas_call(
         functools.partial(gather_kernel, d),
         out_shape=jax.ShapeDtypeStruct((d.m, d.con * d.rows + d.s + 8, d.w), f32),
@@ -337,17 +397,18 @@
         pltpu.VMEM((2 * d.s, d.cols), jnp.bfloat16),
         pltpu.VMEM((1, d.cols), i32),
         pltpu.VMEM((1, d.cols), i32),
+        pltpu.VMEM((d.cw, d.s), f32),
     ]
     slot = jax.ShapeDtypeStruct((d.m, d.s, d.pw), f32)
     part, ints, divisor = pl.pallas_call(
         functools.partial(first_kernel, d),
         grid=(d.rs,),
         out_shape=(jax.ShapeDtypeStruct(piece, f32), slot, slot),
-        in_specs=[SMEM, VMEM, VMEM, VMEM, VMEM, ladder_spec],
+        in_specs=[SMEM, SMEM, VMEM, VMEM, VMEM, VMEM, ladder_spec],
         out_specs=(out_spec, VMEM, VMEM),
         scratch_shapes=keep,
         compiler_params=limit,
-    )(info, got, wide_label, wide_energy, col_label, ladder)
+    )(info, spans, got, wide_label, wide_energy, col_label, ladder)
 
     for repeat in range(ITERS):
         if repeat > 0:
@@ -355,11 +416,11 @@
                 functools.partial(next_kernel, d),
                 grid=(d.rs,),
                 out_shape=jax.ShapeDtypeStruct(piece, f32),
-                in_specs=[SMEM, VMEM, VMEM, VMEM, VMEM, ladder_spec],
+                in_specs=[SMEM, SMEM, VMEM, VMEM, VMEM, VMEM, ladder_spec],
                 out_specs=out_spec,
                 scratch_shapes=keep,
                 compiler_params=limit,
-            )(info, summed, ints, divisor, col_label, ladder)
+            )(info, spans, summed, ints, divisor, col_label, ladder)
         summed = pl.pallas_call(
             functools.partial(reduce_kernel, d),
             out_shape=jax.ShapeDtypeStruct((d.m,) + piece, f32),
@@ -368,10 +429,10 @@
             scratch_shapes=[
                 pltpu.VMEM((d.rs - 1, d.s, d.cw), f32),
                 pltpu.VMEM((d.con, d.s, d.cw), f32),
-                pltpu.SemaphoreType.DMA((d.rs - 1,)),
-                pltpu.SemaphoreType.DMA((d.rs - 1,)),
-                pltpu.SemaphoreType.DMA((d.con,)),
-                pltpu.SemaphoreType.DMA((d.m, d.rs)),
+                pltpu.SemaphoreType.DMA((PARTS, d.rs - 1)),
+                pltpu.SemaphoreType.DMA((PARTS, d.rs - 1)),
+                pltpu.SemaphoreType.DMA((PARTS, d.con)),
+                pltpu.SemaphoreType.DMA((PARTS, d.m, d.rs)),
             ]
             + line_sems,
             compiler_params=pltpu.CompilerParams(

time: 103 us -> 98.3 us (0.954)
  Pallas kernels: 97.3 us -> 88.5 us
  local copies, waits for them, and re-layouts: 4.34 us -> 7.2 us
    pallas_call x2, Pallas kernels: 47.9 us -> 42.1 us  [per_device(): pl.pallas_call(functools.partial(reduce_kernel, d), out_shape=jax.ShapeDt...]
    pallas_call x1, Pallas kernels: 19.2 us -> 16.5 us  [per_device(): pl.pallas_call(functools.partial(gather_kernel, d), out_shape=jax.ShapeDt...]
    slice x0 -> x1, local copies, waits for them, and re-layouts: none -> 1.43 us  [cuts(): jnp.pad(values, (0, count * size - values.shape[0]), mode='edge')]
    concatenate x0 -> x2, local copies, waits for them, and re-layouts: none -> 1.35 us  [cuts(): jnp.pad(values, (0, count * size - values.shape[0]), mode='edge')]
where the time goes in v2:
time: 98.3 us; the launch traced here: 97.3 us
  Pallas kernels  88.5 us (90%)
  local copies, waits for them, and re-layouts  7.2 us (7%)
  other arithmetic  1.54 us (2%)
    pallas_call x2, Pallas kernels, per_device(): pl.pallas_call(functools.partial(reduce_kernel, d), out_shape=jax.ShapeDt...  42.1 us
    pallas_call x1, Pallas kernels, per_device(): pl.pallas_call(functools.partial(gather_kernel, d), out_shape=jax.ShapeDt...  16.5 us
    pallas_call x1, Pallas kernels, per_device(): pl.pallas_call(functools.partial(first_kernel, d), grid=(d.rs,), out_shap...  13.6 us
    pallas_call x1, Pallas kernels, per_device(): pl.pallas_call(functools.partial(next_kernel, d), grid=(d.rs,), out_shape...  12.8 us
    pallas_call x1, Pallas kernels, per_device(): pl.pallas_call(functools.partial(final_kernel, d), out_shape=jax.ShapeDty...  2.27 us

profile of v2, /device:TPU:0, one launch (start us, length us, event | category | flops | bytes accessed | tf_op | source)
XLA Modules:
  0.0 97.3 jit_solution(2458987456411716526)
XLA Ops:
  0.0 0.8 dynamic-slice_bitcast_fusion
  0.8 1.4 %fusion.2 = (s32[1]{0:T(128)}, s32[1]{0:T(128)}) fusion(s32[9600]{0:T(1024)} %param.13, s32[]{:T(128)S(6)} %add.40, s32[]{:T(128)S(6)} %add.41), kind=kLoop, calls=%fused_computation.21 | loop fusion | bytes 24 | tf_op jit(solution)/shard_map/jit(_pad)/slice | solution.py:354
  2.2 0.9 convert_reduce_fusion.3
  3.1 0.7 reshape.66
  3.8 0.9 fusion.3
  4.7 0.2 convert_reduce_fusion
  4.9 0.7 concatenate.16
  5.6 0.1 reshape.65
  5.7 0.2 fusion.1
  5.9 0.1 broadcast_minimum_fusion
  6.0 0.7 concatenate.15
  6.6 0.1 fusion
  6.8 0.1 add_bitcast_fusion
  6.9 0.1 copy.10.label_ref.row_label
  7.0 0.7 copy.11.energy_ref
  7.7 0.0 copy-start
  7.7 1.1 %copy-done = f32[64,2400]{1,0:T(8,128)S(1)} copy-done((f32[64,2400]{1,0:T(8,128)S(1)}, f32[64,2400]{1,0:T(8,128)}, u32[]{:S(2)}) %copy-start) | copy-done | bytes 614424
  8.8 1.3 %shard_map.64.x_ref = f32[1,64,640]{2,1,0:T(8,128)S(1)} custom-call(s32[5,8]{1,0:T(8,128)S(1)} %scatter-min.4.tiles.info, f32[64,2400]{1,0:T(8,128)S(1)} %copy-done, s32[64,1]{1,0:T(8,128)S(1)} %copy.10.label_ref.row_label, f32[64,1]{1,0:T(8,128)S(1)} %copy.11.energy_ref), custom_call_target="tpu_custom_call" | custom-call | tf_op jit(solution)/shard_map/pallas_call | solution.py:370
  10.1 16.5 %shard_map.65.got_ref = f32[1,312,640]{2,1,0:T(8,128)S(1)} custom-call(f32[1,64,640]{2,1,0:T(8,128)S(1)} %shard_map.64.x_ref), custom_call_target="tpu_custom_call" | custom-call | tf_op jit(solution)/shard_map/pallas_call | solution.py:380
  26.5 13.6 %shard_map.66 = (f32[4,48,640]{2,1,0:T(8,128)S(1)}, f32[1,48,3072]{2,1,0:T(8,128)S(1)}, f32[1,48,3072]{2,1,0:T(8,128)S(1)}) custom-call(s32[5,8]{1,0:T(8,128)S(1)} %scatter-min.4.tiles.info, s32[2,18]{1,0:T(2,128)S(1)} %pad_add_fusion.spans, f32[1,312,640]{2,1,0:T(8,128)S(1)} %shard_map.65.got_ref, s32[1,1,3072]{2,1,0:T(1,128)S(1)} %pad_bitcast_fusion.1.wide_label, ...), custom_call_target="tpu_custom_call" | custom-call | tf_op jit(solution)/shard_map/pallas_call | solution.py:403
  40.1 20.5 %shard_map.67.sum_ref = f32[1,4,48,640]{3,2,1,0:T(8,128)S(1)} custom-call(f32[4,48,640]{2,1,0:T(8,128)S(1)} %get-tuple-element.20.x_ref), custom_call_target="tpu_custom_call" | custom-call | tf_op jit(solution)/shard_map/pallas_call | solution.py:424
  60.6 12.8 %shard_map.68.x_ref = f32[4,48,640]{2,1,0:T(8,128)S(1)} custom-call(s32[5,8]{1,0:T(8,128)S(1)} %scatter-min.4.tiles.info, s32[2,18]{1,0:T(2,128)S(1)} %pad_add_fusion.spans, f32[1,4,48,640]{3,2,1,0:T(8,128)S(1)} %shard_map.67.sum_ref, f32[1,48,3072]{2,1,0:T(8,128)S(1)} %get-tuple-element.21.ints_ref, f32[1,48,3072]{2,1,0:T(8,128)S(1)} %get-tuple-element.22.div_ref, ...), custom_call_target="tpu_custom_call" | custom-call | tf_op jit(solution)/shard_map/pallas_call | solution.py:415
  73.4 21.6 %shard_map.69.sum_ref = f32[1,4,48,640]{3,2,1,0:T(8,128)S(1)} custom-call(f32[4,48,640]{2,1,0:T(8,128)S(1)} %shard_map.68.x_ref), custom_call_target="tpu_custom_call" | custom-call | tf_op jit(solution)/shard_map/pallas_call | solution.py:424
  95.1 2.3 %shard_map.70 = f32[64,2400]{1,0:T(8,128)} custom-call(s32[5,8]{1,0:T(8,128)S(1)} %scatter-min.4.tiles.info, f32[1,4,48,640]{3,2,1,0:T(8,128)S(1)} %shard_map.69.sum_ref, f32[1,48,3072]{2,1,0:T(8,128)S(1)} %get-tuple-element.21.ints_ref, f32[1,48,3072]{2,1,0:T(8,128)S(1)} %get-tuple-element.22.div_ref, s32[1,1,3072]{2,1,0:T(1,128)S(1)} %pad_bitcast_fusion.1.wide_label, ...), custom_call_target="tpu_custom_call" | custom-call | tf_op jit(solution)/shard_map/pallas_call | solution.py:443
  (11 shorter events, 0.1 us)
Async XLA Ops:
  7.7 1.1 %copy-start = (f32[64,2400]{1,0:T(8,128)S(1)}, f32[64,2400]{1,0:T(8,128)}, u32[]{:S(2)}) copy-start(f32[64,2400]{1,0:T(8,128)} %x_ref.1) | copy-start | bytes 1843204

commit v3 on v2

--- a/solution.py
+++ b/solution.py
@@ -11,6 +11,7 @@
 LABELS = 8
 PARTS = 2
 CHUNK = 256
+STREAMS = 4
 MESH = pl.DeviceIdType.MESH
 VMEM = pl.BlockSpec(memory_space=pltpu.VMEM)
 SMEM = pl.BlockSpec(memory_space=pltpu.SMEM)
@@ -204,12 +205,12 @@
         copy.wait_send()
 
 
-def product(d, spans, ladder_ref, out_ref, high_low, low, high, acc):
+def product(d, spans, ladder_refs, out_ref, high_low, low, high, acc):
     step = pl.program_id(0)
     dims = (((1,), (1,)), ((), ()))
     acc[...] = jnp.zeros_like(acc)
-    for half in range(2):
-        mine = d.chunks + step * 2 + half
+    for half in range(STREAMS):
+        mine = d.chunks + step * STREAMS + half
         here = pl.ds(half * d.half, d.half)
         for chunk in range(d.chunks):
             cut = slice(chunk * CHUNK, min((chunk + 1) * CHUNK, d.cols))
@@ -219,7 +220,7 @@
                 row = lax.broadcasted_iota(jnp.int32, (d.half, cut.stop - cut.start), 0)
                 row = row + (step * d.cw + half * d.half)
                 keep = (row >= low[:, cut]) & (row < high[:, cut])
-                value = jnp.where(keep, ladder_ref[here, cut], 0.0)
+                value = jnp.where(keep, ladder_refs[half][:, cut], 0.0)
                 value_high = value.astype(jnp.bfloat16)
                 value_low = (value - value_high.astype(jnp.float32)).astype(jnp.bfloat16)
                 first = lax.dot_general(
@@ -249,7 +250,7 @@
 
 
 def first_kernel(
-    d, info, spans, got_ref, wide_label, wide_energy, label_ref, ladder_ref,
+    d, info, spans, got_ref, wide_label, wide_energy, label_ref, l0, l1, l2, l3,
     out_ref, ints_ref, div_ref, amp, high_low, low, high, acc,
 ):
     @pl.when(pl.program_id(0) == 0)
@@ -273,7 +274,7 @@
             amp[:, b * d.v : (b + 1) * d.v] = ints_ref[b, :, : d.v] / div_ref[b, :, : d.v]
         prepare(d, info, label_ref, amp, high_low, low, high)
 
-    product(d, spans, ladder_ref, out_ref, high_low, low, high, acc)
+    product(d, spans, (l0, l1, l2, l3), out_ref, high_low, low, high, acc)
 
 
 def update(d, b, sum_ref, ints_ref, div_ref):
@@ -282,7 +283,7 @@
 
 
 def next_kernel(
-    d, info, spans, sum_ref, ints_ref, div_ref, label_ref, ladder_ref,
+    d, info, spans, sum_ref, ints_ref, div_ref, label_ref, l0, l1, l2, l3,
     out_ref, amp, high_low, low, high, acc,
 ):
     @pl.when(pl.program_id(0) == 0)
@@ -291,7 +292,7 @@
             amp[:, b * d.v : (b + 1) * d.v] = update(d, b, sum_ref, ints_ref, div_ref)[:, : d.v]
         prepare(d, info, label_ref, amp, high_low, low, high)
 
-    product(d, spans, ladder_ref, out_ref, high_low, low, high, acc)
+    product(d, spans, (l0, l1, l2, l3), out_ref, high_low, low, high, acc)
 
 
 def final_kernel(d, info, sum_ref, ints_ref, div_ref, wide_label, row_label, out_ref, slots, wide):
@@ -347,14 +348,14 @@
     )
     info = jnp.minimum(info, jnp.where(jnp.arange(d.m + 4)[:, None] < 2, 1 << 20, d.v))
     info = info.at[2 : 2 + d.m].min(d.v - 1)
-    d.half = d.cw // 2
+    d.half = d.cw // STREAMS
     d.chunks = pl.cdiv(d.cols, CHUNK)
 
     def cuts(values, count, size):
         return jnp.pad(values, (0, count * size - values.shape[0]), mode="edge").reshape(count, size)
 
     by_chunk = cuts(virt_local, d.chunks, CHUNK)
-    by_half = cuts(virt_own, 2 * d.rs, d.half)
+    by_half = cuts(virt_own, STREAMS * d.rs, d.half)
     spans = jnp.stack(
         [
             jnp.concatenate([by_chunk.min(axis=1), by_half.min(axis=1)]),
@@ -389,8 +390,14 @@
     )(packed)
 
     piece = (d.rs, d.s, d.cw)
-    last_block = pl.cdiv(d.v, d.cw) - 1
-    ladder_spec = pl.BlockSpec((d.cw, d.cols), lambda i: (jnp.minimum(i, last_block), 0))
+    last_block = pl.cdiv(d.v, d.half) - 1
+
+    def ladder_spec(k):
+        return pl.BlockSpec(
+            (d.half, d.cols), lambda i: (jnp.minimum(i * STREAMS + k, last_block), 0)
+        )
+
+    ladder_specs = [ladder_spec(k) for k in range(STREAMS)]
     out_spec = pl.BlockSpec((1, d.s, d.cw), lambda i: (i, 0, 0))
     keep = [
         pltpu.VMEM((d.s, d.cols), f32),
@@ -404,11 +411,11 @@
         functools.partial(first_kernel, d),
         grid=(d.rs,),
         out_shape=(jax.ShapeDtypeStruct(piece, f32), slot, slot),
-        in_specs=[SMEM, SMEM, VMEM, VMEM, VMEM, VMEM, ladder_spec],
+        in_specs=[SMEM, SMEM, VMEM, VMEM, VMEM, VMEM, *ladder_specs],
         out_specs=(out_spec, VMEM, VMEM),
         scratch_shapes=keep,
         compiler_params=limit,
-    )(info, spans, got, wide_label, wide_energy, col_label, ladder)
+    )(info, spans, got, wide_label, wide_energy, col_label, *[ladder] * STREAMS)
 
     for repeat in range(ITERS):
         if repeat > 0:
@@ -416,11 +423,11 @@
                 functools.partial(next_kernel, d),
                 grid=(d.rs,),
                 out_shape=jax.ShapeDtypeStruct(piece, f32),
-                in_specs=[SMEM, SMEM, VMEM, VMEM, VMEM, VMEM, ladder_spec],
+                in_specs=[SMEM, SMEM, VMEM, VMEM, VMEM, VMEM, *ladder_specs],
                 out_specs=out_spec,
                 scratch_shapes=keep,
                 compiler_params=limit,
-            )(info, spans, summed, ints, divisor, col_label, ladder)
+            )(info, spans, summed, ints, divisor, col_label, *[ladder] * STREAMS)
         summed = pl.pallas_call(
             functools.partial(reduce_kernel, d),
             out_shape=jax.ShapeDtypeStruct((d.m,) + piece, f32),

time: 98.3 us -> 105 us (1.068)
  Pallas kernels: 88.5 us -> 95.5 us
    pallas_call x1, Pallas kernels: 13.6 us -> 17.9 us  [per_device(): pl.pallas_call(functools.partial(first_kernel, d), grid=(d.rs,), out_shap...]
    pallas_call x1, Pallas kernels: 12.8 us -> 17.1 us  [per_device(): pl.pallas_call(functools.partial(next_kernel, d), grid=(d.rs,), out_shape...]
    pallas_call x2, Pallas kernels: 42.1 us -> 40.5 us  [per_device(): pl.pallas_call(functools.partial(reduce_kernel, d), out_shape=jax.ShapeDt...]
where the time goes in v3:
time: 105 us; the launch traced here: 104 us
  Pallas kernels  95.5 us (91%)
  local copies, waits for them, and re-layouts  7.2 us (7%)
  other arithmetic  1.51 us (1%)
    pallas_call x2, Pallas kernels, per_device(): pl.pallas_call(functools.partial(reduce_kernel, d), out_shape=jax.ShapeDt...  40.5 us
    pallas_call x1, Pallas kernels, per_device(): pl.pallas_call(functools.partial(first_kernel, d), grid=(d.rs,), out_shap...  17.9 us
    pallas_call x1, Pallas kernels, per_device(): pl.pallas_call(functools.partial(next_kernel, d), grid=(d.rs,), out_shape...  17.1 us
    pallas_call x1, Pallas kernels, per_device(): pl.pallas_call(functools.partial(gather_kernel, d), out_shape=jax.ShapeDt...  16.5 us
    pallas_call x1, Pallas kernels, per_device(): pl.pallas_call(functools.partial(final_kernel, d), out_shape=jax.ShapeDty...  2.26 us

profile of v3, /device:TPU:0, one launch (start us, length us, event | category | flops | bytes accessed | tf_op | source)
XLA Modules:
  0.0 104.3 jit_solution(10173333544706125007)
XLA Ops:
  0.0 0.8 dynamic-slice_bitcast_fusion
  0.8 1.4 %fusion.2 = (s32[1]{0:T(128)}, s32[1]{0:T(128)}) fusion(s32[9600]{0:T(1024)} %param.13, s32[]{:T(128)S(6)} %add.40, s32[]{:T(128)S(6)} %add.41), kind=kLoop, calls=%fused_computation.21 | loop fusion | bytes 24 | tf_op jit(solution)/shard_map/jit(_pad)/slice | solution.py:355
  2.2 0.9 convert_reduce_fusion.3
  3.1 0.7 reshape.66
  3.8 0.9 fusion.3
  4.7 0.2 convert_reduce_fusion
  4.9 0.7 concatenate.16
  5.6 0.1 broadcast_minimum_fusion
  5.7 0.1 reshape.65
  5.8 0.1 fusion.1
  5.9 0.7 concatenate.15
  6.6 0.1 fusion
  6.7 0.1 add_bitcast_fusion
  6.8 0.1 copy.10.label_ref.row_label
  6.9 0.7 copy.11.energy_ref
  7.7 0.0 copy-start
  7.7 1.1 %copy-done = f32[64,2400]{1,0:T(8,128)S(1)} copy-done((f32[64,2400]{1,0:T(8,128)S(1)}, f32[64,2400]{1,0:T(8,128)}, u32[]{:S(2)}) %copy-start) | copy-done | bytes 614424
  8.8 1.3 %shard_map.64.x_ref = f32[1,64,640]{2,1,0:T(8,128)S(1)} custom-call(s32[5,8]{1,0:T(8,128)S(1)} %scatter-min.4.tiles.info, f32[64,2400]{1,0:T(8,128)S(1)} %copy-done, s32[64,1]{1,0:T(8,128)S(1)} %copy.10.label_ref.row_label, f32[64,1]{1,0:T(8,128)S(1)} %copy.11.energy_ref), custom_call_target="tpu_custom_call" | custom-call | tf_op jit(solution)/shard_map/pallas_call | solution.py:371
  10.0 16.5 %shard_map.65.got_ref = f32[1,312,640]{2,1,0:T(8,128)S(1)} custom-call(f32[1,64,640]{2,1,0:T(8,128)S(1)} %shard_map.64.x_ref), custom_call_target="tpu_custom_call" | custom-call | tf_op jit(solution)/shard_map/pallas_call | solution.py:381
  26.5 17.9 %shard_map.66 = (f32[4,48,640]{2,1,0:T(8,128)S(1)}, f32[1,48,3072]{2,1,0:T(8,128)S(1)}, f32[1,48,3072]{2,1,0:T(8,128)S(1)}) custom-call(s32[5,8]{1,0:T(8,128)S(1)} %scatter-min.4.tiles.info, s32[2,26]{1,0:T(2,128)S(1)} %pad_add_fusion.spans, f32[1,312,640]{2,1,0:T(8,128)S(1)} %shard_map.65.got_ref, s32[1,1,3072]{2,1,0:T(1,128)S(1)} %pad_bitcast_fusion.1.wide_label, ...), custom_call_target="tpu_custom_call" | custom-call | tf_op jit(solution)/shard_map/pallas_call | solution.py:410
  44.4 19.8 %shard_map.67.sum_ref = f32[1,4,48,640]{3,2,1,0:T(8,128)S(1)} custom-call(f32[4,48,640]{2,1,0:T(8,128)S(1)} %get-tuple-element.20.x_ref), custom_call_target="tpu_custom_call" | custom-call | tf_op jit(solution)/shard_map/pallas_call | solution.py:431
  64.2 17.1 %shard_map.68.x_ref = f32[4,48,640]{2,1,0:T(8,128)S(1)} custom-call(s32[5,8]{1,0:T(8,128)S(1)} %scatter-min.4.tiles.info, s32[2,26]{1,0:T(2,128)S(1)} %pad_add_fusion.spans, f32[1,4,48,640]{3,2,1,0:T(8,128)S(1)} %shard_map.67.sum_ref, f32[1,48,3072]{2,1,0:T(8,128)S(1)} %get-tuple-element.21.ints_ref, f32[1,48,3072]{2,1,0:T(8,128)S(1)} %get-tuple-element.22.div_ref, ...), custom_call_target="tpu_custom_call" | custom-call | tf_op jit(solution)/shard_map/pallas_call | solution.py:422
  81.3 20.8 %shard_map.69.sum_ref = f32[1,4,48,640]{3,2,1,0:T(8,128)S(1)} custom-call(f32[4,48,640]{2,1,0:T(8,128)S(1)} %shard_map.68.x_ref), custom_call_target="tpu_custom_call" | custom-call | tf_op jit(solution)/shard_map/pallas_call | solution.py:431
  102.0 2.3 %shard_map.70 = f32[64,2400]{1,0:T(8,128)} custom-call(s32[5,8]{1,0:T(8,128)S(1)} %scatter-min.4.tiles.info, f32[1,4,48,640]{3,2,1,0:T(8,128)S(1)} %shard_map.69.sum_ref, f32[1,48,3072]{2,1,0:T(8,128)S(1)} %get-tuple-element.21.ints_ref, f32[1,48,3072]{2,1,0:T(8,128)S(1)} %get-tuple-element.22.div_ref, s32[1,1,3072]{2,1,0:T(1,128)S(1)} %pad_bitcast_fusion.1.wide_label, ...), custom_call_target="tpu_custom_call" | custom-call | tf_op jit(solution)/shard_map/pallas_call | solution.py:450
  (11 shorter events, 0.1 us)
Async XLA Ops:
  7.7 1.1 %copy-start = (f32[64,2400]{1,0:T(8,128)S(1)}, f32[64,2400]{1,0:T(8,128)}, u32[]{:S(2)}) copy-start(f32[64,2400]{1,0:T(8,128)} %x_ref.1) | copy-start | bytes 1843204
